TPU v7x, 32 devices: a whole 2x2x4 slice. The times are simulated.
32 devices in a mesh: row: 4 (over y, core), col: 8 (over z, x).
Axes of the slice: x: 2, y: 2, z: 4, core: 2. Of those that a mesh axis runs over, the one named last changes fastest.
Arguments:
- density: float32 [256, 256, 128], P('row', 'col'), may hold values from 0 to 40, as said below
Outputs:
- coarse: float32 [256, 256, 128], P('row', 'col')
- moments: float32 [3, 4, 1, 1], replicated
Inputs may be any that keep to these rules, and one draw needn't show every extreme that they name: Positive density.
All inputs are finite; a program needn't handle non-finite values.
Results may differ from a plain program's by a relative error of at most 0.0003.
Values sent between devices are 32-bit elements; how exact they have to be, the bound alone decides.
A program may use at most 64 MiB of HBM per device.

v0:
```python
import jax
import jax.numpy as jnp
import ml_dtypes
import numpy as np
from jax import lax
from jax.experimental import pallas as pl
from jax.experimental.pallas import tpu as pltpu
from jax.sharding import PartitionSpec as P

SUB = 256


SPLINE_TAPS = (0.0625, 0.25, 0.375, 0.25, 0.0625)
SPACINGS = (4, 8, 16)
EPSILON = 1e-06


def padded_2(block, sides, width):
    for axis, dim in sides:
        count = lax.axis_size(axis)
        forward = [(i, i + 1) for i in range(count - 1)]
        forward.append((count - 1, 0))
        backward = [(target, source) for source, target in forward]
        low = lax.ppermute(
            lax.slice_in_dim(block, block.shape[dim] - width, None, axis=dim), axis, forward
        )
        high = lax.ppermute(lax.slice_in_dim(block, 0, width, axis=dim), axis, backward)
        block = jnp.concatenate([low, block, high], axis=dim)
    return block


def holed_pass(padded, spacing, axis_number, length_out):
    summed = SPLINE_TAPS[0] * lax.slice_in_dim(padded, 0, length_out, axis=axis_number)
    for tap_index in (1, 2, 3, 4):
        portion = lax.slice_in_dim(
            padded, tap_index * spacing, tap_index * spacing + length_out, axis=axis_number
        )
        summed = summed + SPLINE_TAPS[tap_index] * portion
    return summed


def depth_pass(values_in, spacing):
    summed = SPLINE_TAPS[2] * values_in
    for tap_index in (0, 1, 3, 4):
        summed = summed + SPLINE_TAPS[tap_index] * jnp.roll(
            values_in, -(tap_index - 2) * spacing, axis=2
        )
    return summed


def moment_planes(detail):
    square = detail * detail
    return jnp.stack(
        [
            jnp.sum(jnp.abs(detail), axis=2),
            jnp.sum(square, axis=2),
            jnp.sum(square * detail, axis=2),
            jnp.sum(square * square, axis=2),
        ]
    )


def finish_table(table, planes):
    means = table / jnp.float32(SUB * SUB * planes)
    second = means[:, 1]
    third = means[:, 2] / (second + EPSILON) ** 1.5
    fourth = means[:, 3] / (second + EPSILON) ** 2
    return jnp.stack([means[:, 0], second, third, fourth], axis=1)


def per_device(density):
    size_x, size_y, planes = density.shape
    plane_list = []
    current = density
    for spacing in SPACINGS:
        rows_padded = padded_2(current, (("row", 0),), 2 * spacing)
        along_x = holed_pass(rows_padded, spacing, 0, size_x)
        cols_padded = padded_2(along_x, (("col", 1),), 2 * spacing)
        along_y = holed_pass(cols_padded, spacing, 1, size_y)
        smoother = depth_pass(along_y, spacing)
        plane_list.append(moment_planes(current - smoother))
        current = smoother
    planes_all = jnp.stack(plane_list)
    count_x = lax.axis_size("row") * size_x // SUB
    count_y = lax.axis_size("col") * size_y // SUB
    rows_global = lax.axis_index("row") * size_x + jnp.arange(size_x, dtype=jnp.int32)
    cols_global = lax.axis_index("col") * size_y + jnp.arange(size_y, dtype=jnp.int32)
    onehot_x = (
        (rows_global // SUB)[:, None] == jnp.arange(count_x, dtype=jnp.int32)[None, :]
    ).astype(jnp.float32)
    onehot_y = (
        (cols_global // SUB)[:, None] == jnp.arange(count_y, dtype=jnp.int32)[None, :]
    ).astype(jnp.float32)
    partial_table = jnp.einsum(
        "xa,skxy,yb->skab", onehot_x, planes_all, onehot_y, precision=lax.Precision.HIGHEST
    )
    table = lax.psum(partial_table, ("row", "col"))
    return (current, finish_table(table, planes))


MESH = pl.DeviceIdType.MESH
ROWS, COLS = 4, 8
DEVICES = ROWS * COLS
BLOCK = (64, 32, 128)
CLASS_X, CLASS_Y, LANES = 64, 64, 128
CHUNKS = 2


def five_taps(low2, low1, mid, high1, high2):
    return (
        SPLINE_TAPS[0] * (low2 + high2) + SPLINE_TAPS[1] * (low1 + high1) + SPLINE_TAPS[2] * mid
    )


def roll(v, shift, axis):
    shift = shift % v.shape[axis]
    return pltpu.roll(v, shift, axis) if shift else v


KEPT = 100
SPARE = LANES - KEPT
REST = KEPT - 3 * SPARE


def range_matrices():
    cells = np.arange(32)
    columns = [np.full(32, np.sqrt(1 / 32))]
    for m in range(1, 16):
        if m % 4:
            angle = 2 * np.pi * m * cells / 32
            columns += [np.sqrt(1 / 16) * np.cos(angle), np.sqrt(1 / 16) * np.sin(angle)]
    basis = np.kron(np.stack(columns, axis=1), np.eye(4))
    whole = np.zeros((LANES, LANES))
    whole[:, :KEPT] = basis
    spare = [np.zeros((LANES, LANES)) for _ in range(3)]
    for j in range(3):
        spare[j][:, KEPT:] = basis[:, SPARE * j : SPARE * (j + 1)]
    rest = np.tile(basis[:, 3 * SPARE :], (1, LANES // REST))

    def thrice(matrix):
        high = matrix.astype(ml_dtypes.bfloat16)
        low = (matrix - high.astype(np.float64)).astype(ml_dtypes.bfloat16)
        return [high, high, low]

    parts = []
    for j in range(3):
        parts += thrice(whole) + thrice(spare[j])
    parts += thrice(rest)
    parts += thrice(whole.T)
    for j in range(3):
        parts += thrice(spare[j].T)
    parts += thrice(rest.T)
    return np.concatenate(parts, axis=0)


INTO, INTO_REST, OUT, OUT_LAST, MATRIX_ROWS = 0, 2304, 2688, 3072, 4608


def thirds(v):
    high = v.astype(jnp.bfloat16)
    low = (v - high.astype(jnp.float32)).astype(jnp.bfloat16)
    return [high, low, high]


def exchange_pair(lane, distance, first, second):
    clear = (lane & distance) == 0
    return (
        jnp.where(clear, first, roll(second, distance, 2)),
        jnp.where(clear, roll(first, -distance, 2), second),
    )


def class_kernel(
    x_hbm,
    basis_hbm,
    out_ref,
    tab_ref,
    x_ref,
    send,
    f0,
    f1,
    back,
    padded,
    taps,
    basis,
    packed,
    rests,
    sums,
    ssem,
    rsem,
    bssem,
    brsem,
    mssem,
    mrsem,
    xsem,
    basis_sem,
):
    row, col = lax.axis_index("row"), lax.axis_index("col")
    me = row * COLS + col
    col_hi, col_lo = lax.div(col, 2), lax.rem(col, 2)

    order = jnp.where(
        col_hi == 0, 30, jnp.where(col_hi == 1, 180, jnp.where(col_hi == 2, 75, 225))
    )

    planes = [lax.rem(lax.div(order, 4**step), 4) for step in range(4)]

    def each_other(visit):
        for hi in planes:

            @pl.loop(0, ROWS)
            def _(near):
                r = row + near
                r = jnp.where(r >= ROWS, r - ROWS, r)
                visit(r, 2 * hi + 1 - col_lo)

                @pl.when(r * COLS + 2 * hi + col_lo != me)
                def _():
                    visit(r, 2 * hi + col_lo)

    def place(ref, h, r, c):
        return ref.at[h, 4 * r, c]

    def load_x(rx):
        return pltpu.make_async_copy(x_hbm.at[:, rx], x_ref.at[:, rx], xsem.at[rx])

    for rx in range(4):
        load_x(rx).start()
    load_basis = pltpu.make_async_copy(basis_hbm, basis, basis_sem)
    load_basis.start()

    def times(parts, begin):
        left = jnp.concatenate(parts, axis=1)
        right = basis[begin : begin + left.shape[1], :]
        return jnp.dot(left, right, preferred_element_type=jnp.float32)

    barrier = pltpu.get_barrier_semaphore()

    each_other(
        lambda r, c: pl.semaphore_signal(
            barrier, inc=1, device_id=(r, c), device_id_type=MESH
        )
    )

    lane3 = lax.broadcasted_iota(jnp.int32, (4, 8, LANES), 2)

    def pack(h):
        @pl.loop(0, 4)
        def _(rx):
            if h == 0:
                load_x(rx).wait()
            for ry in range(4):
                v = [
                    jnp.stack([x_ref[4 * q + i, rx, pl.ds(ry, 8, stride=4), :] for i in range(4)])
                    for q in range(4)
                ]
                u0 = exchange_pair(lane3, 2, v[0], v[2])[h]
                u1 = exchange_pair(lane3, 2, v[1], v[3])[h]
                w0, w1 = exchange_pair(lane3, 1, u0, u1)
                send[h, rx * COLS + 2 * ry] = w0
                send[h, rx * COLS + 2 * ry + 1] = w1

    def forward(h, r, c, source_r, source_c):
        k = r * COLS + c
        return pltpu.make_async_remote_copy(
            src_ref=send.at[h, k],
            dst_ref=place(f0, h, source_r, source_c),
            send_sem=ssem.at[h],
            recv_sem=rsem.at[h],
            device_id=(r, c),
            device_id_type=MESH,
        )

    def send_all(h):
        each_other(lambda r, c: forward(h, r, c, row, col).start())
        f0[h, 4 * row, col] = send[h, me]

    def wait_bytes(ref, sem):
        pltpu.make_async_copy(ref, ref, sem).wait()

    others = pl.ds(0, DEVICES - 1)

    lane2 = lax.broadcasted_iota(jnp.int32, (CLASS_Y, LANES), 1)
    lane = lax.broadcasted_iota(jnp.int32, (1, LANES), 1)
    begin = REST * lax.broadcasted_iota(jnp.int32, (8, 8, LANES), 1)
    lane_8 = lax.broadcasted_iota(jnp.int32, (8, 8, LANES), 2)
    own_lanes = (lane_8 >= begin) & (lane_8 < begin + REST)

    def fill(ref, h, unit):
        for r in range(4):
            for i in range(4):
                here = ref[h, 4 * r, :, i].reshape(CLASS_Y, LANES)
                after = ref[h, 4 * ((r + 1) % 4), :, i].reshape(CLASS_Y, LANES)
                for m in (1, 2, 3):
                    reached = (i < 2 * unit, unit == 4, i >= 4 - 2 * unit)[m - 1]
                    if reached:
                        ref[h, 4 * r + m, :, i] = jnp.where(
                            (lane2 & 3) < 4 - m, roll(here, -m, 1), roll(after, 4 - m, 1)
                        ).reshape(8, 8, LANES)

    def make_taps():
        shape = (2 * LANES, LANES)
        gap = (
            lax.broadcasted_iota(jnp.int32, shape, 0) - lax.broadcasted_iota(jnp.int32, shape, 1)
        ) & (LANES - 1)
        for scale, spacing in enumerate(SPACINGS):
            matrix = jnp.zeros(shape, jnp.float32)
            for k, tap in zip(range(-2, 3), SPLINE_TAPS):
                matrix = jnp.where(gap == (k * spacing) % LANES, tap, matrix)
            taps[scale] = matrix.astype(jnp.bfloat16)

    def smooth_rows(src, dst, h, scale, r, acc):
        unit = SPACINGS[scale] // 4
        mids = []
        for i in range(4):

            def at(k):
                n = i + k * unit
                block = 4 * r + n // 4
                block = jnp.where(block < 0, block + 16, jnp.where(block >= 16, block - 16, block))
                return src[h, block, :, n % 4].reshape(CLASS_Y, LANES)

            mids.append(at(0))
            v = five_taps(at(-2), at(-1), mids[i], at(1), at(2))
            padded[i, 8:72, :] = v
            padded[i, 0:8, :] = v[56:]
            padded[i, 72:80, :] = v[:8]
        rows = []
        for i in range(4):
            rows.append(
                five_taps(*(padded[i, 8 + k * unit : 72 + k * unit, :] for k in range(-2, 3)))
            )
        v = jnp.concatenate(rows, axis=0)
        high = v.astype(jnp.bfloat16)
        low = (v - high.astype(jnp.float32)).astype(jnp.bfloat16)
        v = jnp.dot(
            jnp.concatenate([high, low], axis=1), taps[scale], preferred_element_type=jnp.float32
        )
        for i in range(4):
            smooth = v[CLASS_Y * i : CLASS_Y * (i + 1)]
            if scale < len(SPACINGS) - 1:
                dst[h, 4 * r, :, i] = smooth.reshape(8, 8, LANES)
            detail = (mids[i] - smooth).reshape(8, 8, LANES)
            square = detail * detail
            parts = (jnp.abs(detail), square, square * detail, square * square)
            acc = tuple(s + jnp.sum(p, axis=0) for s, p in zip(acc, parts))
        if scale == len(SPACINGS) - 1:
            last = v[3 * CLASS_Y :]
            for j in range(3):
                row_j = v[CLASS_Y * j : CLASS_Y * (j + 1)]
                t = times(thirds(row_j) + thirds(last), INTO + 768 * j)
                packed[h, pl.ds(8 * r, 8), j] = t.reshape(8, 8, LANES)
            t = times(thirds(last), INTO_REST).reshape(8, 8, LANES)
            t = jnp.sum(jnp.where(own_lanes, t, 0.0), axis=1)
            for c in range(COLS):
                rests[8 * r + c, h] = t[c : c + 1]
        return acc

    def backward(h, r, c, source_r, source_c):
        source = source_r * COLS + source_c
        return pltpu.make_async_remote_copy(
            src_ref=packed.at[h, r * COLS + c],
            dst_ref=back.at[h, source],
            send_sem=bssem.at[h],
            recv_sem=brsem.at[h, source_r],
            device_id=(r, c),
            device_id_type=MESH,
        )

    def scales(h, accs):
        fields = (f0, f1, f0, f1)
        results = []
        for scale, spacing in enumerate(SPACINGS):
            src, dst = fields[scale], fields[scale + 1]
            fill(src, h, spacing // 4)

            acc = accs[scale]
            for near in range(4):
                r = row + near
                r = jnp.where(r >= ROWS, r - ROWS, r)
                acc = smooth_rows(src, dst, h, scale, r, acc)
                if scale == len(SPACINGS) - 1:
                    for hi in planes:
                        for c in (2 * hi + 1 - col_lo, 2 * hi + col_lo):

                            @pl.when(r * COLS + c != me)
                            def _():
                                backward(h, r, c, row, col).start()

            results.append(acc)
        back[h, me] = packed[h, me]
        return results

    make_taps()
    pack(0)
    pl.semaphore_wait(barrier, DEVICES - 1)
    send_all(0)
    pack(1)
    send_all(1)
    accs = [(jnp.zeros((8, LANES), jnp.float32),) * 4] * len(SPACINGS)

    def chunk(h, accs):
        wait_bytes(send.at[h, others], rsem.at[h])
        return scales(h, accs)

    load_basis.wait()
    accs = lax.fori_loop(0, CHUNKS, chunk, accs)

    total = jnp.zeros((1, LANES), jnp.float32)
    for scale, acc in enumerate(accs):
        for moment, s in enumerate(acc):
            value = jnp.sum(jnp.sum(s, axis=0, keepdims=True), axis=1, keepdims=True)
            total = total + jnp.where(lane == 4 * scale + moment, value, 0.0)
    for k in range(DEVICES):
        rests[k, 2] = total
    sums[me] = rests[me]

    def share(r, c, source):
        return pltpu.make_async_remote_copy(
            src_ref=rests.at[r * COLS + c],
            dst_ref=sums.at[source],
            send_sem=mssem,
            recv_sem=mrsem,
            device_id=(r, c),
            device_id_type=MESH,
        )

    each_other(lambda r, c: share(r, c, me).start())

    def wait_back(h, rx):
        @pl.when(rx == row)
        def _():
            wait_bytes(packed.at[h, pl.ds(0, COLS - 1)], brsem.at[h, rx])

        @pl.when(rx != row)
        def _():
            wait_bytes(packed.at[h, pl.ds(0, COLS)], brsem.at[h, rx])

    def back_thirds(h, rx):
        return [thirds(back[h, pl.ds(8 * rx, 8), k].reshape(CLASS_Y, LANES)) for k in range(3)]

    @pl.loop(0, 4)
    def _(j):
        rx = row - j
        rx = jnp.where(rx < 0, rx + ROWS, rx)
        wait_back(0, rx)
        parts = back_thirds(0, rx)
        for k in range(3):
            f0[0, rx, :, k] = times(parts[k], OUT).reshape(8, 8, LANES)
        f0[0, rx, :, 3] = times(sum(parts, []), OUT_LAST).reshape(8, 8, LANES)

    wait_bytes(sums.at[others], mrsem)

    @pl.loop(0, 4)
    def _(j):
        rx = lax.rem(row + 4 - j, 4)
        wait_back(1, rx)
        rows = []
        for h in range(CHUNKS):
            rest = jnp.stack([jnp.broadcast_to(sums[8 * rx + c, h], (8, LANES)) for c in range(COLS)])
            rest = thirds(jnp.where(own_lanes, rest, 0.0).reshape(CLASS_Y, LANES))
            if h == 0:
                lines = [f0[0, rx, :, k].reshape(CLASS_Y, LANES) for k in range(4)]
                lines[3] = lines[3] + times(rest, OUT_LAST + 1152)
            else:
                parts = back_thirds(h, rx)
                lines = [times(t, OUT) for t in parts] + [times(sum(parts, []) + rest, OUT_LAST)]
            rows.append(lines)
        for ry in range(4):
            u = []
            for h in range(CHUNKS):
                w = [
                    jnp.stack([v[8 * c : 8 * c + 8] for v in rows[h]])
                    for c in (2 * ry, 2 * ry + 1)
                ]
                u.append(exchange_pair(lane3, 1, w[0], w[1]))
            for q in range(2):
                for low, v in enumerate(exchange_pair(lane3, 2, u[0][q], u[1][q])):
                    for i in range(4):
                        out_ref[4 * (q + 2 * low) + i, rx, pl.ds(ry, 8, stride=4), :] = v[i]

    wait_bytes(sums.at[others], mssem)
    for h in range(CHUNKS):
        wait_bytes(send.at[h, others], ssem.at[h])
        wait_bytes(packed.at[h, others], bssem.at[h])

    means = sum(sums[k, 2] for k in range(DEVICES)) / jnp.float32(SUB * SUB * LANES)
    moment = lane & 3
    second = jnp.where(moment == 2, roll(means, 1, 1), roll(means, 2, 1)) + EPSILON
    power = second * jnp.where(moment == 2, jnp.sqrt(second), second)
    final = jnp.where(moment < 2, means, means / power)
    for scale in range(len(SPACINGS)):
        tab_ref[scale] = final[:, 4 * scale : 4 * scale + 4]


def per_device_classes(density):
    size_x, size_y, planes = density.shape
    dma = pltpu.SemaphoreType.DMA((CHUNKS,))
    block = pltpu.VMEM((CHUNKS, DEVICES, 4, 8, LANES), jnp.float32)
    part = pltpu.VMEM((CHUNKS, DEVICES, 3, 8, LANES), jnp.float32)
    rests = pltpu.VMEM((DEVICES, 3, 1, LANES), jnp.float32)
    field = pltpu.VMEM((CHUNKS, CLASS_X // 4, CLASS_Y // 8, 4, 8, LANES), jnp.float32)
    coarse, moments = pl.pallas_call(
        class_kernel,
        out_shape=(
            jax.ShapeDtypeStruct((16, 4, size_y, planes), jnp.float32),
            jax.ShapeDtypeStruct((len(SPACINGS), 1, 4), jnp.float32),
        ),
        in_specs=[pl.BlockSpec(memory_space=pltpu.HBM)] * 2,
        out_specs=(pl.BlockSpec(memory_space=pltpu.VMEM),) * 2,
        scratch_shapes=[
            pltpu.VMEM((16, 4, size_y, planes), jnp.float32),
            block,
            field,
            field,
            part,
            pltpu.VMEM((4, CLASS_Y + 16, LANES), jnp.float32),
            pltpu.VMEM((len(SPACINGS), 2 * LANES, LANES), jnp.bfloat16),
            pltpu.VMEM((MATRIX_ROWS, LANES), jnp.bfloat16),
            part,
            rests,
            rests,
        ]
        + [dma] * 3
        + [pltpu.SemaphoreType.DMA((CHUNKS, ROWS))]
        + [pltpu.SemaphoreType.DMA] * 2
        + [pltpu.SemaphoreType.DMA((4,)), pltpu.SemaphoreType.DMA],
        compiler_params=pltpu.CompilerParams(
            collective_id=0, has_side_effects=True, vmem_limit_bytes=32 * 1024 * 1024
        ),
    )(
        pltpu.with_memory_space_constraint(density.reshape(16, 4, size_y, planes), pltpu.HBM),
        pltpu.with_memory_space_constraint(jnp.asarray(range_matrices()), pltpu.HBM),
    )
    return coarse.reshape(size_x, size_y, planes), moments.reshape(len(SPACINGS), 4, 1, 1)


def solution(mesh):
    placed = (P("row", "col", None),)

    def program(density):
        size_x, size_y, planes = density.shape
        local = (size_x // mesh.shape["row"], size_y // mesh.shape["col"], planes)
        classes = (mesh.shape["row"], mesh.shape["col"]) == (ROWS, COLS) and local == BLOCK
        return jax.shard_map(
            per_device_classes if classes else per_device,
            mesh=mesh,
            in_specs=placed,
            out_specs=(P("row", "col", None), P()),
            check_vma=False,
        )(density)

    return program
```

profile of v0, /device:TPU:0, one launch (start us, length us, event | category | flops | bytes accessed | tf_op | source)
XLA Modules:
  0.0 54.1 jit_solution(4261407686557019444)
XLA Ops:
  0.6 51.9 %shard_map.41 = (f32[16,4,32,128]{3,2,1,0:T(8,128)S(1)}, f32[3,1,4]{2,1,0:T(1,128)S(1)}) custom-call(f32[16,4,32,128]{3,2,1,0:T(8,128)} %bitcast.7, bf16[4608,128]{1,0:T(8,128)(2,1)} %constant.2.clone.basis_hbm), custom_call_target="tpu_custom_call" | custom-call | tf_op jit(solution)/shard_map/pallas_call | solution.py:503
  52.6 1.0 %copy.7 = f32[64,32,128]{2,1,0:T(8,128)} copy(f32[64,32,128]{2,1,0:T(8,128)S(1)} %bitcast.5) | data formatting | bytes 2097152
  53.5 0.6 %copy.8 = f32[3,4,1,1]{1,3,2,0:T(1,128)} copy(f32[3,4,1,1]{1,3,2,0:T(1,128)S(1)} %bitcast.6) | data formatting | bytes 96
where the time goes:
time: 54.3 us; the launch traced here: 54.1 us
  Pallas kernels  51.9 us (96%)
  local copies, waits for them, and re-layouts  1.53 us (3%)
  between operations  0.64 us (1%)
    pallas_call x1, Pallas kernels, per_device_classes(): pl.pallas_call(class_kernel, out_shape=(jax.ShapeDtypeStruct((16, 4, size...  51.9 us
    unnamed x2, local copies, waits for them, and re-layouts  1.53 us

commit v1 on v0

--- a/solution.py
+++ b/solution.py
@@ -206,13 +206,13 @@
     planes = [lax.rem(lax.div(order, 4**step), 4) for step in range(4)]
 
     def each_other(visit):
-        for hi in planes:
-
-            @pl.loop(0, ROWS)
-            def _(near):
-                r = row + near
-                r = jnp.where(r >= ROWS, r - ROWS, r)
+        @pl.loop(0, ROWS)
+        def _(near):
+            r = row + near
+            r = jnp.where(r >= ROWS, r - ROWS, r)
+            for hi in planes:
                 visit(r, 2 * hi + 1 - col_lo)
+            for hi in planes:
 
                 @pl.when(r * COLS + 2 * hi + col_lo != me)
                 def _():

time: 54.3 us -> 53.5 us (0.985)
  Pallas kernels: 51.9 us -> 51.1 us
    pallas_call x1, Pallas kernels: 51.9 us -> 51.1 us  [per_device_classes(): pl.pallas_call(class_kernel, out_shape=(jax.ShapeDtypeStruct((16, 4, size...]
where the time goes in v1:
time: 53.5 us; the launch traced here: 53.3 us
  Pallas kernels  51.1 us (96%)
  local copies, waits for them, and re-layouts  1.53 us (3%)
  between operations  0.64 us (1%)
    pallas_call x1, Pallas kernels, per_device_classes(): pl.pallas_call(class_kernel, out_shape=(jax.ShapeDtypeStruct((16, 4, size...  51.1 us
    unnamed x2, local copies, waits for them, and re-layouts  1.53 us

profile of v1, /device:TPU:0, one launch (start us, length us, event | category | flops | bytes accessed | tf_op | source)
XLA Modules:
  0.0 53.3 jit_solution(15248684801094420173)
XLA Ops:
  0.6 51.1 %shard_map.41 = (f32[16,4,32,128]{3,2,1,0:T(8,128)S(1)}, f32[3,1,4]{2,1,0:T(1,128)S(1)}) custom-call(f32[16,4,32,128]{3,2,1,0:T(8,128)} %bitcast.7, bf16[4608,128]{1,0:T(8,128)(2,1)} %constant.2.clone.basis_hbm), custom_call_target="tpu_custom_call" | custom-call | tf_op jit(solution)/shard_map/pallas_call | solution.py:503
  51.8 1.0 %copy.7 = f32[64,32,128]{2,1,0:T(8,128)} copy(f32[64,32,128]{2,1,0:T(8,128)S(1)} %bitcast.5) | data formatting | bytes 2097152
  52.8 0.6 %copy.8 = f32[3,4,1,1]{1,3,2,0:T(1,128)} copy(f32[3,4,1,1]{1,3,2,0:T(1,128)S(1)} %bitcast.6) | data formatting | bytes 96
